TPU v7x, 512 devices: a whole 4x4x16 slice. The times are simulated.
512 devices in a mesh: va: 32 (over x, z_lo), vb: 16 (over y, z_hi, core).
Axes of the slice: x: 4, y: 4, z: 16 (z_hi: 2, z_lo: 8; z = z_hi * 8 + z_lo), core: 2. Of those that a mesh axis runs over, the one named last changes fastest.
Arguments:
- lam: bfloat16 [4, 6144, 6144], P(None, 'va', 'vb'), may hold values from -6 to 6
- fock_vv: bfloat16 [6144, 6144], P('va', 'vb'), may hold values from -0.078125 to 0.078125
- amp: bfloat16 [4, 6144, 6144], P(None, 'va', 'vb'), may hold values from -6 to 6
- tile_mask: int32 [4, 64, 64], P(None, 'va', 'vb'), may hold values 0 or 1
- integrals: bfloat16 [4, 6144, 6144], P(None, 'va', 'vb'), may hold values from -6 to 6
Outputs:
- residual: bfloat16 [4, 6144, 6144], P(None, 'va', 'vb')
All inputs are finite; a program needn't handle non-finite values. No bound on the sum of `tile_mask` on one device may be relied on, other than what follows from the above.
Results may differ from a plain program's by a relative error of at most 0.001.
Values may be sent and summed in bfloat16 or wider, within the bound.
A program may use at most 64 MiB of HBM per device.

v0:
```python
import jax
import jax.numpy as jnp
from jax import lax
from jax.sharding import PartitionSpec as P

VIRT = 6144


def body(lam, fock_vv, amp, tile_mask, integrals):
    pair_count = lam.shape[0]
    tile_size = lam.shape[1] // tile_mask.shape[1]
    widened = jnp.repeat(jnp.repeat(tile_mask, tile_size, axis=1), tile_size, axis=2)
    screened = amp * widened.astype(jnp.bfloat16)
    local_intersection = jnp.dot(
        lam.reshape(pair_count, -1),
        screened.reshape(pair_count, -1).T,
        preferred_element_type=jnp.float32,
    )
    summed = lax.psum(local_intersection, ("va", "vb"))
    intersection = summed / VIRT
    ladder = jnp.einsum(
        "pq,qab->pab", intersection, integrals.astype(jnp.float32), precision=lax.Precision.HIGHEST
    )
    fock_cols = lax.all_gather(fock_vv, "va", axis=0, tiled=True)
    one_body = jnp.einsum(
        "pad,db->pab",
        lax.all_gather(lam, "vb", axis=2, tiled=True),
        fock_cols,
        preferred_element_type=jnp.float32,
    )
    total_sum = integrals.astype(jnp.float32) + one_body + ladder
    return total_sum.astype(jnp.bfloat16)


def solution(mesh):
    in_specs = (
        P(None, "va", "vb"),
        P("va", "vb"),
        P(None, "va", "vb"),
        P(None, "va", "vb"),
        P(None, "va", "vb"),
    )
    out_specs = P(None, "va", "vb")
    return jax.shard_map(body, mesh=mesh, in_specs=in_specs, out_specs=out_specs, check_vma=False)
```

profile of v0, /device:TPU:1, one launch (start us, length us, event | category | flops | bytes accessed | tf_op | source)
XLA Modules:
  0.0 464.6 jit_solution(10144468208986921496)
XLA Ops:
  6.5 0.0 copy-start
  6.5 0.0 copy-start.1
  6.5 0.0 all-gather.5.cloned.1.call-start
  6.5 0.7 all-gather.5.cloned.1.call-update
  7.3 0.0 all-gather.3.cloned.1.call-start
  7.3 0.7 all-gather.3.cloned.1.call-update
  8.0 0.7 convert_element_type.19
  8.7 1.0 broadcast_in_dim.7
  9.7 0.5 convert_element_type.21
  10.2 1.2 mul.3
  11.5 0.0 copy-done
  11.5 0.9 convolution_bitcast_fusion
  12.4 112.4 %psum.7 = f32[4,4]{1,0:T(4,128)S(1)} all-reduce(f32[4,4]{1,0:T(4,128)S(1)} %convolution_bitcast_fusion), channel_id=1, replica_groups=mesh['va'=32,'vb'=16] {'va','vb'}, use_global_device_ids=true, to_apply=%region_0.0 | all-reduce | flops 16 | bytes 128 | tf_op jit(solution)/shard_map/psum | solution.py:19
  124.7 0.0 copy-done.1
  124.7 1.2 fusion.11
  125.9 109.7 %all-gather.5.cloned.1.call-done = bf16[6144,384]{1,0:T(8,128)(2,1)} async-done(((bf16[192,384]{1,0:T(8,128)(2,1)}), bf16[6144,384]{1,0:T(8,128)(2,1)}) %all-gather.5.cloned.1.call-update) | async-done | bytes 4718608 | tf_op jit(solution)/shard_map/all_gather | solution.py:24
  235.6 212.4 %all-gather.3.cloned.1.call-done = bf16[4,192,6144]{2,1,0:T(8,128)(2,1)} async-done(((bf16[4,192,384]{2,1,0:T(8,128)(2,1)}), bf16[4,192,6144]{2,1,0:T(8,128)(2,1)}) %all-gather.3.cloned.1.call-update) | async-done | bytes 9437200 | tf_op jit(solution)/shard_map/all_gather | solution.py:27
  448.0 9.8 %fusion.8 = bf16[4,192,384]{2,1,0:T(8,128)(2,1)} fusion(bf16[4,192,6144]{2,1,0:T(8,128)(2,1)} %all-gather.3.cloned.1.call-done, bf16[6144,384]{1,0:T(8,128)(2,1)} %all-gather.5.cloned.1.call-done, f32[4,192,384]{2,0,1:T(4,128)S(1)} %fusion.11, bf16[4,192,384]{2,1,0:T(8,128)(2,1)S(1)} %copy-done.1), kind=kOutput, calls=%fused_computation.4 | convolution fusion | flops 3625058304 | bytes 16515072 | tf_op jit(solution)/shard_map/pad,db->pab/dot_general | solution.py:25
  (1 shorter events, 0.0 us)
Async XLA Ops:
  6.5 4.9 %copy-start = (bf16[4,192,384]{2,1,0:T(8,128)(2,1)S(1)}, bf16[4,192,384]{2,1,0:T(8,128)(2,1)}, u32[]{:S(2)}) copy-start(bf16[4,192,384]{2,1,0:T(8,128)(2,1)} %param.5) | copy-start | bytes 1769476
  6.5 118.2 %copy-start.1 = (bf16[4,192,384]{2,1,0:T(8,128)(2,1)S(1)}, bf16[4,192,384]{2,1,0:T(8,128)(2,1)}, u32[]{:S(2)}) copy-start(bf16[4,192,384]{2,1,0:T(8,128)(2,1)} %param.9) | copy-start | bytes 1769476
  6.5 229.1 %all-gather.5.cloned.1.call-start = ((), (), s32[]{:S(2)}) async-start(), calls=%async_computation.1 | async-start | bytes 4866048 | tf_op jit(solution)/shard_map/all_gather | solution.py:24
  7.3 440.7 %all-gather.3.cloned.1.call-start = ((), (), s32[]{:S(2)}) async-start(), calls=%async_computation | async-start | bytes 10027008 | tf_op jit(solution)/shard_map/all_gather | solution.py:27
Sparse Core Ops, SparseCore 0:
  9.4 226.1 all-gather.4
  238.7 209.2 all-gather.2
where the time goes:
time: 471 us; the launch traced here: 465 us
  waiting for transfers between devices  324 us (69%)
  blocking collectives  112 us (24%)
  between operations  13.4 us (3%)
  matrix products  11.8 us (3%)
    all_gather x1, waiting for transfers between devices, body(): lax.all_gather(lam, 'vb', axis=2, tiled=True)  212 us
    psum x1, blocking collectives, body(): summed = lax.psum(local_intersection, ('va', 'vb'))  112 us
    all_gather x1, waiting for transfers between devices, body(): fock_cols = lax.all_gather(fock_vv, 'va', axis=0, tiled=True)  110 us
    dot_general x1, matrix products, body(): jnp.einsum('pad,db->pab', lax.all_gather(lam, 'vb', axis=2, tiled=True),...  9.77 us
  transfers between devices with their start and end apart: 2, of which 2 were waited for; matrix products, arithmetic and copies ran while one was open for 1% of the time, Pallas kernels for 0%

commit v1 on v0

v1 whole, which is shorter than its diff:
```python
import functools

import jax
import jax.numpy as jnp
from jax import lax
from jax.experimental import pallas as pl
from jax.experimental.pallas import tpu as pltpu
from jax.sharding import PartitionSpec as P

VIRT = 6144
PAIRS = 4
RA = 192
CB = 384
ROWS = PAIRS * RA
HALF = RA // 2
MESH = pl.DeviceIdType.MESH

NU = 4
LAM_START = (0, 3, 6, 9)
FOCK_START = (0, 2)
STEPS = LAM_START[-1] + 8

SUM_STEPS = (
    (0, 0, 0, 1),
    (0, 1, 0, 0),
    (0, 2, 0, 0),
    (1, 0, 0, 0),
    (2, 0, 0, 0),
    (0, 0, 1, 0),
    (0, 0, 2, 0),
    (0, 0, 4, 0),
    (0, 0, 8, 0),
)


def kernel(
    lam_ref, fock_ref, amp_ref, mask_ref, int_ref, out_ref,
    L, F, T, A, I, acc, O, sbuf, rbuf,
    in_sem, lam_rs, fock_rs, fock_ss, x_rs, y0_rs, y1_rs, c0_rs, c1_rs, sum_rs, sum_ss,
    zs_sem, xs_sem, ys_sem, cs_sem, out_sem,
):
    va, vb = lax.axis_index("va"), lax.axis_index("vb")
    x, zl = va // 8, va % 8
    y, zh, c = vb // 4, (vb // 2) % 2, vb % 2
    z = zh * 8 + zl

    def dev(dx, dy, dz, dc):
        xx, yy, zz, cc = (x + dx) % 4, (y + dy) % 4, (z + dz) % 16, (c + dc) % 2
        return (xx * 8 + zz % 8, (yy * 2 + zz // 8) * 2 + cc)

    def remote(src, dst, ss, rs, to):
        pltpu.make_async_remote_copy(src, dst, ss, rs, device_id=dev(*to), device_id_type=MESH).start()

    def wait(ref, sem):
        pltpu.make_async_copy(ref, ref, sem).wait()

    own = vb
    far = (y * 2 + (1 - zh)) * 2 + c

    def frows(zsrc, f=None):
        base = (x * 8 + zsrc) * RA
        if f is None:
            return F.at[pl.ds(pl.multiple_of(base, RA), RA)]
        return F.at[pl.ds(pl.multiple_of(base + f * HALF, HALF), HALF)]

    def lrows(b, u, d):
        return L.at[b, pl.ds(u * RA + d * HALF, HALF)]

    cp_lam = pltpu.make_async_copy(lam_ref, L.at[own], in_sem.at[0])
    cp_fock = pltpu.make_async_copy(fock_ref, frows(zl), in_sem.at[1])
    cp_amp = pltpu.make_async_copy(amp_ref, A, in_sem.at[2])
    cp_int = pltpu.make_async_copy(int_ref, I, in_sem.at[3])
    cp_lam.start()
    cp_fock.start()
    cp_amp.start()
    cp_int.start()

    peers = set()
    for o in SUM_STEPS + ((0, 3, 0, 0), (3, 0, 0, 0), (0, 0, 15, 0)):
        peers.add(o)
        peers.add(((-o[0]) % 4, (-o[1]) % 4, (-o[2]) % 16, (-o[3]) % 2))
    peers = sorted(peers)
    bar = pltpu.get_barrier_semaphore()
    for o in peers:
        pl.semaphore_signal(bar, inc=1, device_id=dev(*o), device_id_type=MESH)
    pl.semaphore_wait(bar, len(peers))

    DZ = ((0, 0, 1, 0), (0, 0, -1, 0))
    SG = (1, -1)

    def lam_send(d, u, h):
        src = lrows(own, u, d) if h == 0 else T.at[d, u, h - 1]
        if h < 7:
            dst = T.at[d, u, h]
        else:
            zz = (z + SG[d]) % 16
            dst = lrows((y * 2 + (1 - zz // 8)) * 2 + c, u, d)
        remote(src, dst, zs_sem, lam_rs.at[d, u, h], DZ[d])

    def lam_wait(d, u, h):
        wait(T.at[d, u, h] if h < 7 else lrows(far, u, d), lam_rs.at[d, u, h])

    def fock_send(d, f, h):
        s = SG[d]
        zsrc = zl - s * h

        @pl.when((zsrc >= 0) & (zsrc < 8) & (zl + s >= 0) & (zl + s < 8))
        def _():
            blk = frows(zsrc, f)
            remote(blk, blk, fock_ss.at[d, f, h], fock_rs.at[d, f, h], DZ[d])

    def fock_arrive(d, f, h):
        s = SG[d]
        zsrc = zl - s * (h + 1)

        @pl.when((zsrc >= 0) & (zsrc < 8))
        def _():
            blk = frows(zsrc, f)
            wait(blk, fock_rs.at[d, f, h])

        if h < 6:
            fock_send(d, f, h + 1)

        @pl.when((zsrc >= 0) & (zsrc < 8))
        def _():
            blk = frows(zsrc, f)
            for dx in (1, 3, 2):
                remote(blk, blk, xs_sem, x_rs, (dx, 0, 0, 0))

    cp_lam.wait()
    cp_fock.wait()
    for u in range(NU):
        if LAM_START[u] == 0:
            for d in (0, 1):
                lam_send(d, u, 0)
    for f in (0, 1):
        if FOCK_START[f] == 0:
            for d in (0, 1):
                fock_send(d, f, 0)
    blk = frows(zl)
    for dx in (1, 3, 2):
        remote(blk, blk, xs_sem, x_rs, (dx, 0, 0, 0))
    for dy in (1, 3, 2):
        remote(L.at[own], L.at[own], ys_sem, y0_rs.at[dy - 1], (0, dy, 0, 0))
    remote(L.at[own], L.at[own], cs_sem, c0_rs, (0, 0, 0, 1))

    cp_amp.wait()
    col = lax.broadcasted_iota(jnp.int32, (1, CB), 1) // HALF
    row8 = lax.broadcasted_iota(jnp.int32, (8, 128), 0)
    col8 = lax.broadcasted_iota(jnp.int32, (8, 128), 1)
    part = jnp.zeros((8, 128), jnp.float32)
    for q in range(PAIRS):
        sums = tuple(jnp.zeros((16, CB), jnp.float32) for _ in range(PAIRS))
        for i in range(2):
            wide = jnp.zeros((1, CB), jnp.float32)
            for j in range(4):
                kept = mask_ref[q, i, j].astype(jnp.float32)
                wide = wide + kept * (col == j).astype(jnp.float32)

            def rows16(k, sums, i=i, q=q, wide=wide):
                r = pl.multiple_of(i * HALF + k * 16, 16)
                a = A[pl.ds(q * RA + r, 16), :].astype(jnp.float32) * wide
                return tuple(
                    s + L[own, pl.ds(p * RA + r, 16), :].astype(jnp.float32) * a for p, s in enumerate(sums)
                )

            sums = lax.fori_loop(0, HALF // 16, rows16, sums)
        for p in range(PAIRS):
            part = part + jnp.where((row8 == p) & (col8 == q), jnp.sum(sums[p]), 0.0)
    sbuf[0] = part
    remote(sbuf.at[0], rbuf.at[0], sum_ss.at[0], sum_rs.at[0], SUM_STEPS[0])

    def sum_step(k):
        wait(rbuf.at[k], sum_rs.at[k])
        sbuf[k + 1] = sbuf[k] + rbuf[k]
        if k + 1 < len(SUM_STEPS):
            remote(sbuf.at[k + 1], rbuf.at[k + 1], sum_ss.at[k + 1], sum_rs.at[k + 1], SUM_STEPS[k + 1])

    def base():
        cp_int.wait()
        inter = sbuf[len(SUM_STEPS)] / VIRT

        def rows16(k, carry):
            r = pl.multiple_of(k * 16, 16)
            g = [I[pl.ds(q * RA + r, 16), :].astype(jnp.float32) for q in range(PAIRS)]
            for p in range(PAIRS):
                t = g[p]
                for q in range(PAIRS):
                    t = t + inter[p : p + 1, q : q + 1] * g[q]
                acc[pl.ds(p * RA + r, 16), :] = t
            return carry

        lax.fori_loop(0, RA // 16, rows16, 0)

    def y0_arrive(dy):
        b = (((y - dy) % 4) * 2 + zh) * 2 + c
        wait(L.at[b], y0_rs.at[dy - 1])
        remote(L.at[b], L.at[b], cs_sem, c0_rs, (0, 0, 0, 1))

    def lam_final(d, u):
        blk = lrows(far, u, d)
        for dy in (1, 3, 2):
            remote(blk, blk, ys_sem, y1_rs.at[d, u, dy - 1], (0, dy, 0, 0))
        remote(blk, blk, cs_sem, c1_rs.at[d, u], (0, 0, 0, 1))

    def y1_arrive(d, u):
        for dy in (1, 3, 2):
            blk = lrows((((y - dy) % 4) * 2 + (1 - zh)) * 2 + c, u, d)
            wait(blk, y1_rs.at[d, u, dy - 1])
            remote(blk, blk, cs_sem, c1_rs.at[d, u], (0, 0, 0, 1))

    def mat(rows, zhalf):
        t = acc[rows, :]
        for yy in range(4):
            b = (yy * 2 + zhalf) * 2
            k = jnp.concatenate([L[b, rows, :], L[b + 1, rows, :]], axis=1)
            w = F[pl.ds(pl.multiple_of(b * CB, 2 * CB), 2 * CB), :]
            t = t + jnp.dot(k, w, preferred_element_type=jnp.float32)
        return t

    extra = {}

    def at(step, fn):
        extra.setdefault(step, []).append(fn)

    for k in range(len(SUM_STEPS)):
        at(k + 1, functools.partial(sum_step, k))
    at(len(SUM_STEPS) + 1, base)
    for i, dy in enumerate((1, 3, 2)):
        at(8 + i, functools.partial(y0_arrive, dy))
    for u in range(NU):
        for d in (0, 1):
            if u < NU - 1:
                at(LAM_START[u] + 8 + 3, functools.partial(y1_arrive, d, u))

    for t in range(1, STEPS + 1):
        for u in range(NU):
            h = t - LAM_START[u]
            if 0 <= h <= 8:
                for d in (0, 1):
                    if h > 0:
                        lam_wait(d, u, h - 1)
                    if h < 8:
                        lam_send(d, u, h)
                    else:
                        lam_final(d, u)
        for f in (0, 1):
            h = t - FOCK_START[f]
            if 0 <= h <= 7:
                for d in (0, 1):
                    if h == 0:
                        fock_send(d, f, 0)
                    else:
                        fock_arrive(d, f, h - 1)
        for fn in extra.pop(t, ()):
            fn()
    for t in sorted(extra):
        for fn in extra[t]:
            fn()

    wait(F.at[pl.ds(0, 24 * RA)], x_rs)
    wait(L.at[pl.ds(0, 4)], c0_rs)

    @pl.loop(0, PAIRS)
    def _(p):
        rows = pl.ds(pl.multiple_of(p * RA, RA), RA)
        acc[rows, :] = mat(rows, zh)

    for u in range(NU):
        if u == NU - 1:
            for d in (0, 1):
                y1_arrive(d, u)
        for d in (0, 1):
            wait(L.at[0, pl.ds(0, 4 * HALF)], c1_rs.at[d, u])
        rows = pl.ds(u * RA, RA)
        O[rows, :] = mat(rows, 1 - zh).astype(jnp.bfloat16)
        pltpu.make_async_copy(O.at[rows], out_ref.at[rows], out_sem.at[u]).start()

    wait(L.at[pl.ds(0, 8)], zs_sem)
    wait(L.at[pl.ds(0, 6)], xs_sem)
    wait(L.at[pl.ds(0, 6)], ys_sem)
    wait(L.at[pl.ds(0, 8)], cs_sem)
    for d in (0, 1):
        s = SG[d]
        for h in range(7):
            zsrc = zl - s * h

            @pl.when((zsrc >= 0) & (zsrc < 8) & (zl + s >= 0) & (zl + s < 8))
            def _(d=d, h=h):
                for f in (0, 1):
                    wait(F.at[pl.ds(0, HALF)], fock_ss.at[d, f, h])

    for k in range(len(SUM_STEPS)):
        wait(sbuf.at[k], sum_ss.at[k])
    for u in range(NU):
        rows = pl.ds(u * RA, RA)
        wait(O.at[rows], out_sem.at[u])


def body(lam, fock_vv, amp, tile_mask, integrals):
    bf16, f32 = jnp.bfloat16, jnp.float32
    dma = pltpu.SemaphoreType.DMA
    n = len(SUM_STEPS)
    anyspec = pl.BlockSpec(memory_space=pl.ANY)
    out = pl.pallas_call(
        kernel,
        name="residual",
        out_shape=jax.ShapeDtypeStruct((ROWS, CB), bf16),
        in_specs=[anyspec, anyspec, anyspec, pl.BlockSpec(memory_space=pltpu.SMEM), anyspec],
        out_specs=anyspec,
        scratch_shapes=[
            pltpu.VMEM((16, ROWS, CB), bf16),
            pltpu.VMEM((VIRT, CB), bf16),
            pltpu.VMEM((2, NU, 7, HALF, CB), bf16),
            pltpu.VMEM((ROWS, CB), bf16),
            pltpu.VMEM((ROWS, CB), bf16),
            pltpu.VMEM((ROWS, CB), f32),
            pltpu.VMEM((ROWS, CB), bf16),
            pltpu.VMEM((n + 1, 8, 128), f32),
            pltpu.VMEM((n, 8, 128), f32),
            dma((4,)),
            dma((2, NU, 8)),
            dma((2, 2, 7)),
            dma((2, 2, 7)),
            dma,
            dma((3,)),
            dma((2, NU, 3)),
            dma,
            dma((2, NU)),
            dma((n,)),
            dma((n,)),
            dma,
            dma,
            dma,
            dma,
            dma((NU,)),
        ],
        compiler_params=pltpu.CompilerParams(
            collective_id=0, has_side_effects=True, vmem_limit_bytes=63 << 20
        ),
    )(lam.reshape(ROWS, CB), fock_vv, amp.reshape(ROWS, CB), tile_mask, integrals.reshape(ROWS, CB))
    return out.reshape(PAIRS, RA, CB)


def solution(mesh):
    split = P(None, "va", "vb")
    return jax.shard_map(
        body, mesh=mesh, in_specs=(split, P("va", "vb"), split, split, split), out_specs=split, check_vma=False
    )
```

time: 471 us -> 133 us (0.28); the launches traced: 465 us -> 133 us
  waiting for transfers between devices: 324 us -> 0 us
  Pallas kernels: 0 us -> 131 us
  blocking collectives: 112 us -> 0 us
  between operations: 13.4 us -> 0.01 us
  matrix products: 11.8 us -> 0 us
    all_gather x2 -> x0, waiting for transfers between devices: 322 us -> none  [the longest x1 212 us: body(): lax.all_gather(lam, 'vb', axis=2, tiled=True)]
    pallas_call x0 -> x1, Pallas kernels: none -> 131 us  [body(): pl.pallas_call(kernel, name='residual', out_shape=jax.ShapeDtypeStruct((R...]
    psum x1 -> x0, blocking collectives: 112 us -> none  [body(): summed = lax.psum(local_intersection, ('va', 'vb'))]
    dot_general x3 -> x0, matrix products: 11.8 us -> none  [the longest x1 9.77 us: body(): jnp.einsum('pad,db->pab', lax.all_gather(lam, 'vb', axis=2, tiled=True),...]
  transfers between devices with their start and end apart: 2 -> 0, of which waited for: 2 -> 0; matrix products, arithmetic and copies ran while one was open for 1% -> 0% of each run, Pallas kernels for 0% -> 0%
where the time goes in v1:
time: 133 us
  Pallas kernels  131 us (98%)
  local copies, waits for them, and re-layouts  1.94 us (1%)
    pallas_call x1, Pallas kernels, body(): pl.pallas_call(kernel, name='residual', out_shape=jax.ShapeDtypeStruct((R...  131 us

profile of v1, /device:TPU:1, one launch (start us, length us, event | category | flops | bytes accessed | tf_op | source)
XLA Modules:
  0.0 132.9 jit_solution(13246935660702232503)
XLA Ops:
  0.0 131.0 %residual.1 = bf16[768,384]{1,0:T(8,128)(2,1)} custom-call(bf16[768,384]{1,0:T(8,128)(2,1)} %bitcast.5, bf16[192,384]{1,0:T(8,128)(2,1)} %fock_ref.1, bf16[768,384]{1,0:T(8,128)(2,1)} %bitcast.6, s32[4,2,4]{2,1,0:T(2,128)} %mask_ref.1, bf16[768,384]{1,0:T(8,128)(2,1)} %bitcast.7), custom_call_target="tpu_custom_call" | custom-call | tf_op jit(solution)/shard_map/residual/pallas_call | solution.py:305
  131.0 1.9 %copy.7 = bf16[4,192,384]{2,1,0:T(8,128)(2,1)} copy(bf16[4,192,384]{2,1,0:T(8,128)(2,1)} %bitcast.4) | data formatting | bytes 1179648

commit v2 on v1

v2 whole, which is shorter than its diff:
```python
import functools

import jax
import jax.numpy as jnp
from jax import lax
from jax.experimental import pallas as pl
from jax.experimental.pallas import tpu as pltpu
from jax.sharding import PartitionSpec as P

VIRT = 6144
PAIRS = 4
RA = 192
CB = 384
ROWS = PAIRS * RA
HALF = RA // 2
MESH = pl.DeviceIdType.MESH

UNITS = ((64, 0), (64, 0), (64, 0), (64, 0), (64, 8), (64, 8))
PARTS = ((64, 0), (64, 7), (64, 8))
Y0_AT = 9
Y1_LAG = 5
INTER_AT = (0.2, 0.4)
SUM_AT = (2.5, 5.5, 8.5, 11.5)
LAST = max(t for _, t in UNITS)
NU, NF = len(UNITS), len(PARTS)
UOFF = tuple(sum(r for r, _ in UNITS[:u]) for u in range(NU + 1))
FOFF = tuple(sum(r for r, _ in PARTS[:f]) for f in range(NF + 1))

SUM_STAGES = (
    tuple((0, dy, 0, dc) for dc in (1, 0) for dy in (0, 1, 3, 2) if dy + dc),
    ((1, 0, 0, 0), (3, 0, 0, 0), (2, 0, 0, 0)),
    ((0, 0, 4, 0), (0, 0, 12, 0), (0, 0, 8, 0)),
    ((0, 0, 1, 0), (0, 0, 15, 0), (0, 0, 2, 0)),
)
NS = len(SUM_STAGES)


def kernel(
    lam_ref, fock_ref, amp_ref, mask_ref, int_ref, out_ref,
    L, F, T, A, I, acc, O, sbuf, rbuf,
    in_sem, lam_rs, fock_rs, fock_ss, x_rs, y0_rs, y1_rs, c0_rs, c1_rs, sum_rs, sum_ss,
    zs_sem, xs_sem, ys_sem, cs_sem, out_sem,
):
    va, vb = lax.axis_index("va"), lax.axis_index("vb")
    x, zl = va // 8, va % 8
    y, zh, c = vb // 4, (vb // 2) % 2, vb % 2
    z = zh * 8 + zl

    def dev(dx, dy, dz, dc):
        xx, yy, zz, cc = (x + dx) % 4, (y + dy) % 4, (z + dz) % 16, (c + dc) % 2
        return (xx * 8 + zz % 8, (yy * 2 + zz // 8) * 2 + cc)

    def remote(src, dst, ss, rs, to):
        pltpu.make_async_remote_copy(src, dst, ss, rs, device_id=dev(*to), device_id_type=MESH).start()

    def wait(ref, sem):
        pltpu.make_async_copy(ref, ref, sem).wait()

    own = vb
    far = (y * 2 + (1 - zh)) * 2 + c

    def frows(zsrc, f=None):
        base = (x * 8 + zsrc) * RA
        if f is None:
            return F.at[pl.ds(pl.multiple_of(base, RA), RA)]
        return F.at[pl.ds(pl.multiple_of(base + FOFF[f], 16), PARTS[f][0])]

    def lrows(b, u, d):
        return L.at[b, pl.ds(2 * UOFF[u] + d * UNITS[u][0], UNITS[u][0])]

    def urows(b, u):
        return L.at[b, pl.ds(2 * UOFF[u], 2 * UNITS[u][0])]

    def transit(d, u, h):
        return T.at[d, h, pl.ds(UOFF[u], UNITS[u][0])]

    cp_lam = pltpu.make_async_copy(lam_ref, L.at[own], in_sem.at[0])
    cp_fock = pltpu.make_async_copy(fock_ref, frows(zl), in_sem.at[1])
    cp_amp = pltpu.make_async_copy(amp_ref, A, in_sem.at[2])
    cp_int = pltpu.make_async_copy(int_ref, I, in_sem.at[3])
    cp_lam.start()
    cp_fock.start()
    cp_amp.start()
    cp_int.start()

    peers = set()
    for o in sum(SUM_STAGES, ()):
        peers.add(o)
        peers.add(((-o[0]) % 4, (-o[1]) % 4, (-o[2]) % 16, (-o[3]) % 2))
    peers = sorted(peers)
    bar = pltpu.get_barrier_semaphore()
    for o in peers:
        pl.semaphore_signal(bar, inc=1, device_id=dev(*o), device_id_type=MESH)
    pl.semaphore_wait(bar, len(peers))

    DZ = ((0, 0, 1, 0), (0, 0, -1, 0))
    SG = (1, -1)

    def lam_send(d, u, h):
        src = lrows(own, u, d) if h == 0 else transit(d, u, h - 1)
        if h < 7:
            dst = transit(d, u, h)
        else:
            zz = (z + SG[d]) % 16
            dst = lrows((y * 2 + (1 - zz // 8)) * 2 + c, u, d)
        remote(src, dst, zs_sem, lam_rs.at[d, u, h], DZ[d])

    def lam_wait(d, u, h):
        wait(transit(d, u, h) if h < 7 else lrows(far, u, d), lam_rs.at[d, u, h])

    def fock_send(d, f, h):
        s = SG[d]
        zsrc = zl - s * h

        @pl.when((zsrc >= 0) & (zsrc < 8) & (zl + s >= 0) & (zl + s < 8))
        def _():
            blk = frows(zsrc, f)
            remote(blk, blk, fock_ss.at[d, f, h], fock_rs.at[d, f, h], DZ[d])

    def fock_arrive(d, f, h):
        s = SG[d]
        zsrc = zl - s * (h + 1)

        @pl.when((zsrc >= 0) & (zsrc < 8))
        def _():
            blk = frows(zsrc, f)
            wait(blk, fock_rs.at[d, f, h])

        if h < 6:
            fock_send(d, f, h + 1)

        @pl.when((zsrc >= 0) & (zsrc < 8))
        def _():
            blk = frows(zsrc, f)
            for dx in (1, 3, 2):
                remote(blk, blk, xs_sem, x_rs, (dx, 0, 0, 0))

    cp_lam.wait()
    for u in range(NU):
        if UNITS[u][1] == 0:
            for d in (0, 1):
                lam_send(d, u, 0)
    cp_fock.wait()
    for f in range(NF):
        if PARTS[f][1] == 0:
            for d in (0, 1):
                fock_send(d, f, 0)
    blk = frows(zl)
    for dx in (1, 3, 2):
        remote(blk, blk, xs_sem, x_rs, (dx, 0, 0, 0))
    remote(L.at[own], L.at[own], cs_sem, c0_rs, (0, 0, 0, 1))
    def inter_part(i):
        if i == 0:
            cp_amp.wait()
        col = lax.broadcasted_iota(jnp.int32, (8, 128), 1)
        wide = []
        for q in range(PAIRS):
            kept = [mask_ref[q, i, j].astype(jnp.float32) for j in range(4)]
            wide.append(
                [jnp.where(col + g * 128 < (g + 1) * HALF, kept[g], kept[g + 1]) for g in range(3)]
            )

        def rows16(k, sums):
            sums = list(sums)
            r = pl.multiple_of(i * HALF + k * 16, 16)
            for g in range(3):
                lanes = pl.ds(g * 128, 128)
                a = [A[pl.ds(q * RA + r, 16), lanes].astype(jnp.float32) for q in range(PAIRS)]
                t = [L[own, pl.ds(p * RA + r, 16), lanes].astype(jnp.float32) for p in range(PAIRS)]
                for e in (0, 8):
                    for q in range(PAIRS):
                        m = a[q][e : e + 8] * wide[q][g]
                        for p in range(PAIRS):
                            sums[q * PAIRS + p] += t[p][e : e + 8] * m
            return tuple(sums)

        zeros = tuple(jnp.zeros((8, 128), jnp.float32) for _ in range(PAIRS * PAIRS))
        sums = lax.fori_loop(0, HALF // 16, rows16, zeros)
        rows = jnp.concatenate([jnp.sum(t, axis=0, keepdims=True) for t in sums], axis=0)
        part = jnp.broadcast_to(jnp.sum(rows, axis=1, keepdims=True), (PAIRS * PAIRS, 128))
        if i == 0:
            sbuf[0] = part
        else:
            sbuf[0] = sbuf[0] + part
            sum_send(0)
            for dy in (1, 3, 2):
                remote(L.at[own], L.at[own], ys_sem, y0_rs.at[dy - 1], (0, dy, 0, 0))

    def sum_send(k):
        for i, o in enumerate(SUM_STAGES[k]):
            remote(sbuf.at[k], rbuf.at[k, i], sum_ss.at[k], sum_rs.at[k], o)

    def sum_arrive(k):
        n = len(SUM_STAGES[k])
        wait(rbuf.at[k, pl.ds(0, n)], sum_rs.at[k])
        t = sbuf[k]
        for i in range(n):
            t = t + rbuf[k, i]
        sbuf[k + 1] = t
        if k + 1 < NS:
            sum_send(k + 1)

    def base():
        cp_int.wait()
        total = sbuf[NS] / VIRT
        inter = [
            [jnp.broadcast_to(total[q * PAIRS + p : q * PAIRS + p + 1, :], (16, 128)) for q in range(PAIRS)]
            for p in range(PAIRS)
        ]

        def rows16(k, carry):
            r = pl.multiple_of(k * 16, 16)
            for g in range(3):
                lanes = pl.ds(g * 128, 128)
                v = [I[pl.ds(q * RA + r, 16), lanes].astype(jnp.float32) for q in range(PAIRS)]
                for p in range(PAIRS):
                    t = v[p]
                    for q in range(PAIRS):
                        t = t + inter[p][q] * v[q]
                    acc[pl.ds(p * RA + r, 16), lanes] = t
            return carry

        lax.fori_loop(0, RA // 16, rows16, 0)

    def y0_arrive(dy):
        b = (((y - dy) % 4) * 2 + zh) * 2 + c
        wait(L.at[b], y0_rs.at[dy - 1])
        remote(L.at[b], L.at[b], cs_sem, c0_rs, (0, 0, 0, 1))

    def lam_final(u):
        blk = urows(far, u)
        for dy in (1, 3, 2):
            remote(blk, blk, ys_sem, y1_rs.at[u, dy - 1], (0, dy, 0, 0))
        remote(blk, blk, cs_sem, c1_rs.at[u], (0, 0, 0, 1))

    def y1_arrive(u):
        for dy in (1, 3, 2):
            blk = urows((((y - dy) % 4) * 2 + (1 - zh)) * 2 + c, u)
            wait(blk, y1_rs.at[u, dy - 1])
            remote(blk, blk, cs_sem, c1_rs.at[u], (0, 0, 0, 1))

    def mat(rows, zhalf):
        t = acc[rows, :]
        for yy in range(4):
            b = (yy * 2 + zhalf) * 2
            k = jnp.concatenate([L[b, rows, :], L[b + 1, rows, :]], axis=1)
            w = F[pl.ds(pl.multiple_of(b * CB, 2 * CB), 2 * CB), :]
            t = t + jnp.dot(k, w, preferred_element_type=jnp.float32)
        return t

    def near():
        wait(F.at[pl.ds(0, 24 * RA)], x_rs)
        wait(L.at[pl.ds(0, 4)], c0_rs)

        @pl.loop(0, PAIRS)
        def _(p):
            rows = pl.ds(pl.multiple_of(p * RA, RA), RA)
            acc[rows, :] = mat(rows, zh)

    def lam_step(u, h):
        for d in (0, 1):
            if h > 0:
                lam_wait(d, u, h - 1)
            if h < 8:
                lam_send(d, u, h)
        if h == 8:
            lam_final(u)

    def fock_step(f, h):
        for d in (0, 1):
            if h == 0:
                fock_send(d, f, 0)
            else:
                fock_arrive(d, f, h - 1)

    events = []

    def at(step, fn, *args):
        events.append((step, len(events), functools.partial(fn, *args)))

    for u in range(NU):
        for h in range(9):
            if UNITS[u][1] + h > 0:
                at(UNITS[u][1] + h, lam_step, u, h)
        at(LAST + 9 if UNITS[u][1] == LAST else UNITS[u][1] + 8 + Y1_LAG, y1_arrive, u)
    for f in range(NF):
        for h in range(8):
            if PARTS[f][1] + h > 0:
                at(PARTS[f][1] + h + 0.1, fock_step, f, h)
    for i in range(2):
        at(INTER_AT[i], inter_part, i)
    for k in range(NS):
        at(SUM_AT[k], sum_arrive, k)
    for i, dy in enumerate((1, 3, 2)):
        at(Y0_AT + 0.3 * i, y0_arrive, dy)
    at(LAST + 8.5, base)
    at(LAST + 8.6, near)
    for _, _, fn in sorted(events, key=lambda e: e[:2]):
        fn()

    for u in range(NU):
        wait(L.at[0, pl.ds(0, 8 * UNITS[u][0])], c1_rs.at[u])
        rows = pl.ds(2 * UOFF[u], 2 * UNITS[u][0])
        O[rows, :] = mat(rows, 1 - zh).astype(jnp.bfloat16)
        pltpu.make_async_copy(O.at[rows], out_ref.at[rows], out_sem.at[u]).start()

    wait(L.at[pl.ds(0, 8)], zs_sem)
    wait(L.at[pl.ds(0, 6)], xs_sem)
    wait(L.at[pl.ds(0, 6)], ys_sem)
    wait(L.at[pl.ds(0, 8)], cs_sem)
    for d in (0, 1):
        s = SG[d]
        for h in range(7):
            zsrc = zl - s * h

            @pl.when((zsrc >= 0) & (zsrc < 8) & (zl + s >= 0) & (zl + s < 8))
            def _(d=d, h=h):
                for f in range(NF):
                    wait(F.at[pl.ds(0, PARTS[f][0])], fock_ss.at[d, f, h])

    for k in range(NS):
        wait(rbuf.at[k, pl.ds(0, len(SUM_STAGES[k]))], sum_ss.at[k])
    for u in range(NU):
        rows = pl.ds(2 * UOFF[u], 2 * UNITS[u][0])
        wait(O.at[rows], out_sem.at[u])


def body(lam, fock_vv, amp, tile_mask, integrals):
    bf16, f32 = jnp.bfloat16, jnp.float32
    dma = pltpu.SemaphoreType.DMA
    anyspec = pl.BlockSpec(memory_space=pl.ANY)
    out = pl.pallas_call(
        kernel,
        name="residual",
        out_shape=jax.ShapeDtypeStruct((ROWS, CB), bf16),
        in_specs=[anyspec, anyspec, anyspec, pl.BlockSpec(memory_space=pltpu.SMEM), anyspec],
        out_specs=anyspec,
        scratch_shapes=[
            pltpu.VMEM((16, ROWS, CB), bf16),
            pltpu.VMEM((VIRT, CB), bf16),
            pltpu.VMEM((2, 7, ROWS // 2, CB), bf16),
            pltpu.VMEM((ROWS, CB), bf16),
            pltpu.VMEM((ROWS, CB), bf16),
            pltpu.VMEM((ROWS, CB), f32),
            pltpu.VMEM((ROWS, CB), bf16),
            pltpu.VMEM((NS + 1, PAIRS * PAIRS, 128), f32),
            pltpu.VMEM((NS, 7, PAIRS * PAIRS, 128), f32),
            dma((4,)),
            dma((2, NU, 8)),
            dma((2, NF, 7)),
            dma((2, NF, 7)),
            dma,
            dma((3,)),
            dma((NU, 3)),
            dma,
            dma((NU,)),
            dma((NS,)),
            dma((NS,)),
            dma,
            dma,
            dma,
            dma,
            dma((NU,)),
        ],
        compiler_params=pltpu.CompilerParams(
            collective_id=0, has_side_effects=True, vmem_limit_bytes=63 << 20
        ),
    )(lam.reshape(ROWS, CB), fock_vv, amp.reshape(ROWS, CB), tile_mask, integrals.reshape(ROWS, CB))
    return out.reshape(PAIRS, RA, CB)


def solution(mesh):
    split = P(None, "va", "vb")
    return jax.shard_map(
        body, mesh=mesh, in_specs=(split, P("va", "vb"), split, split, split), out_specs=split, check_vma=False
    )
```

time: 133 us -> 109 us (0.82)
  Pallas kernels: 131 us -> 107 us
    pallas_call x1, Pallas kernels: 131 us -> 107 us  [body(): pl.pallas_call(kernel, name='residual', out_shape=jax.ShapeDtypeStruct((R...]
where the time goes in v2:
time: 109 us
  Pallas kernels  107 us (98%)
  local copies, waits for them, and re-layouts  1.94 us (2%)
    pallas_call x1, Pallas kernels, body(): pl.pallas_call(kernel, name='residual', out_shape=jax.ShapeDtypeStruct((R...  107 us

profile of v2, /device:TPU:1, one launch (start us, length us, event | category | flops | bytes accessed | tf_op | source)
XLA Modules:
  0.0 108.5 jit_solution(1789008609688730183)
XLA Ops:
  0.0 106.6 %residual.1 = bf16[768,384]{1,0:T(8,128)(2,1)} custom-call(bf16[768,384]{1,0:T(8,128)(2,1)} %bitcast.5, bf16[192,384]{1,0:T(8,128)(2,1)} %fock_ref.1, bf16[768,384]{1,0:T(8,128)(2,1)} %bitcast.6, s32[4,2,4]{2,1,0:T(2,128)} %mask_ref.1, bf16[768,384]{1,0:T(8,128)(2,1)} %bitcast.7), custom_call_target="tpu_custom_call" | custom-call | tf_op jit(solution)/shard_map/residual/pallas_call | solution.py:332
  106.6 1.9 %copy.7 = bf16[4,192,384]{2,1,0:T(8,128)(2,1)} copy(bf16[4,192,384]{2,1,0:T(8,128)(2,1)} %bitcast.4) | data formatting | bytes 1179648

commit v3 on v2

--- a/solution.py
+++ b/solution.py
@@ -15,19 +15,20 @@
 HALF = RA // 2
 MESH = pl.DeviceIdType.MESH
 
-UNITS = ((64, 0), (64, 0), (64, 0), (64, 0), (64, 8), (64, 8))
+UNITS = ((64, 0), (64, 0), (64, 0), (64, 0), (64, 7), (64, 7))
 PARTS = ((64, 0), (64, 7), (64, 8))
 Y0_AT = 9
 Y1_LAG = 5
 INTER_AT = (0.2, 0.4)
-SUM_AT = (2.5, 5.5, 8.5, 11.5)
+SUM_AT = (1.2, 3.5, 6.5, 9.5, 12.5)
 LAST = max(t for _, t in UNITS)
 NU, NF = len(UNITS), len(PARTS)
 UOFF = tuple(sum(r for r, _ in UNITS[:u]) for u in range(NU + 1))
 FOFF = tuple(sum(r for r, _ in PARTS[:f]) for f in range(NF + 1))
 
 SUM_STAGES = (
-    tuple((0, dy, 0, dc) for dc in (1, 0) for dy in (0, 1, 3, 2) if dy + dc),
+    ((0, 0, 0, 1),),
+    ((0, 1, 0, 0), (0, 3, 0, 0), (0, 2, 0, 0)),
     ((1, 0, 0, 0), (3, 0, 0, 0), (2, 0, 0, 0)),
     ((0, 0, 4, 0), (0, 0, 12, 0), (0, 0, 8, 0)),
     ((0, 0, 1, 0), (0, 0, 15, 0), (0, 0, 2, 0)),
@@ -42,13 +43,26 @@
     zs_sem, xs_sem, ys_sem, cs_sem, out_sem,
 ):
     va, vb = lax.axis_index("va"), lax.axis_index("vb")
-    x, zl = va // 8, va % 8
-    y, zh, c = vb // 4, (vb // 2) % 2, vb % 2
+    x, zl = lax.div(va, 8), lax.rem(va, 8)
+    y, zh, c = lax.div(vb, 4), lax.rem(lax.div(vb, 2), 2), lax.rem(vb, 2)
     z = zh * 8 + zl
+    ids = {}
 
     def dev(dx, dy, dz, dc):
-        xx, yy, zz, cc = (x + dx) % 4, (y + dy) % 4, (z + dz) % 16, (c + dc) % 2
-        return (xx * 8 + zz % 8, (yy * 2 + zz // 8) * 2 + cc)
+        o = (dx, dy, dz, dc)
+        if o not in ids:
+            a, b = va, vb
+            if dx:
+                a = a + (lax.rem(x + dx, 4) - x) * 8
+            if dy:
+                b = b + (lax.rem(y + dy, 4) - y) * 4
+            if dz:
+                zz = lax.rem(z + dz, 16)
+                a, b = a + lax.rem(zz, 8) - zl, b + (lax.div(zz, 8) - zh) * 2
+            if dc:
+                b = b + 1 - 2 * c
+            ids[o] = (a, b)
+        return ids[o]
 
     def remote(src, dst, ss, rs, to):
         pltpu.make_async_remote_copy(src, dst, ss, rs, device_id=dev(*to), device_id_type=MESH).start()
@@ -93,7 +107,7 @@
         pl.semaphore_signal(bar, inc=1, device_id=dev(*o), device_id_type=MESH)
     pl.semaphore_wait(bar, len(peers))
 
-    DZ = ((0, 0, 1, 0), (0, 0, -1, 0))
+    DZ = ((0, 0, 1, 0), (0, 0, 15, 0))
     SG = (1, -1)
 
     def lam_send(d, u, h):
@@ -101,8 +115,8 @@
         if h < 7:
             dst = transit(d, u, h)
         else:
-            zz = (z + SG[d]) % 16
-            dst = lrows((y * 2 + (1 - zz // 8)) * 2 + c, u, d)
+            zz = lax.rem(z + DZ[d][2], 16)
+            dst = lrows((y * 2 + (1 - lax.div(zz, 8))) * 2 + c, u, d)
         remote(src, dst, zs_sem, lam_rs.at[d, u, h], DZ[d])
 
     def lam_wait(d, u, h):
@@ -183,8 +197,6 @@
         else:
             sbuf[0] = sbuf[0] + part
             sum_send(0)
-            for dy in (1, 3, 2):
-                remote(L.at[own], L.at[own], ys_sem, y0_rs.at[dy - 1], (0, dy, 0, 0))
 
     def sum_send(k):
         for i, o in enumerate(SUM_STAGES[k]):
@@ -199,6 +211,9 @@
         sbuf[k + 1] = t
         if k + 1 < NS:
             sum_send(k + 1)
+        if k == 0:
+            for dy in (1, 3, 2):
+                remote(L.at[own], L.at[own], ys_sem, y0_rs.at[dy - 1], (0, dy, 0, 0))
 
     def base():
         cp_int.wait()
@@ -223,7 +238,7 @@
         lax.fori_loop(0, RA // 16, rows16, 0)
 
     def y0_arrive(dy):
-        b = (((y - dy) % 4) * 2 + zh) * 2 + c
+        b = (lax.rem(y + 4 - dy, 4) * 2 + zh) * 2 + c
         wait(L.at[b], y0_rs.at[dy - 1])
         remote(L.at[b], L.at[b], cs_sem, c0_rs, (0, 0, 0, 1))
 
@@ -235,7 +250,7 @@
 
     def y1_arrive(u):
         for dy in (1, 3, 2):
-            blk = urows((((y - dy) % 4) * 2 + (1 - zh)) * 2 + c, u)
+            blk = urows((lax.rem(y + 4 - dy, 4) * 2 + (1 - zh)) * 2 + c, u)
             wait(blk, y1_rs.at[u, dy - 1])
             remote(blk, blk, cs_sem, c1_rs.at[u], (0, 0, 0, 1))
 
@@ -294,7 +309,7 @@
     for i, dy in enumerate((1, 3, 2)):
         at(Y0_AT + 0.3 * i, y0_arrive, dy)
     at(LAST + 8.5, base)
-    at(LAST + 8.6, near)
+    at(max(LAST + 8.6, max(t for _, t in PARTS) + 7.2), near)
     for _, _, fn in sorted(events, key=lambda e: e[:2]):
         fn()
 
@@ -344,7 +359,7 @@
             pltpu.VMEM((ROWS, CB), f32),
             pltpu.VMEM((ROWS, CB), bf16),
             pltpu.VMEM((NS + 1, PAIRS * PAIRS, 128), f32),
-            pltpu.VMEM((NS, 7, PAIRS * PAIRS, 128), f32),
+            pltpu.VMEM((NS, 3, PAIRS * PAIRS, 128), f32),
             dma((4,)),
             dma((2, NU, 8)),
             dma((2, NF, 7)),

time: 109 us -> 109 us (level)
  no operation moved by 1% of the time
where the time goes in v3:
time: 109 us; the launch traced here: 108 us
  Pallas kernels  106 us (97%)
  local copies, waits for them, and re-layouts  1.94 us (2%)
    pallas_call x1, Pallas kernels, body(): pl.pallas_call(kernel, name='residual', out_shape=jax.ShapeDtypeStruct((R...  106 us

profile of v3, /device:TPU:1, one launch (start us, length us, event | category | flops | bytes accessed | tf_op | source)
XLA Modules:
  0.0 108.2 jit_solution(86969446535900377)
XLA Ops:
  0.0 106.3 %residual.1 = bf16[768,384]{1,0:T(8,128)(2,1)} custom-call(bf16[768,384]{1,0:T(8,128)(2,1)} %bitcast.5, bf16[192,384]{1,0:T(8,128)(2,1)} %fock_ref.1, bf16[768,384]{1,0:T(8,128)(2,1)} %bitcast.6, s32[4,2,4]{2,1,0:T(2,128)} %mask_ref.1, bf16[768,384]{1,0:T(8,128)(2,1)} %bitcast.7), custom_call_target="tpu_custom_call" | custom-call | tf_op jit(solution)/shard_map/residual/pallas_call | solution.py:347
  106.3 1.9 %copy.7 = bf16[4,192,384]{2,1,0:T(8,128)(2,1)} copy(bf16[4,192,384]{2,1,0:T(8,128)(2,1)} %bitcast.4) | data formatting | bytes 1179648

commit v4 on v3

--- a/solution.py
+++ b/solution.py
@@ -244,7 +244,7 @@
 
     def lam_final(u):
         blk = urows(far, u)
-        for dy in (1, 3, 2):
+        for dy in (2, 1, 3):
             remote(blk, blk, ys_sem, y1_rs.at[u, dy - 1], (0, dy, 0, 0))
         remote(blk, blk, cs_sem, c1_rs.at[u], (0, 0, 0, 1))
 

time: 109 us -> 108 us (level)
  no operation moved by 1% of the time
where the time goes in v4:
time: 108 us
  Pallas kernels  106 us (98%)
  local copies, waits for them, and re-layouts  1.94 us (2%)
    pallas_call x1, Pallas kernels, body(): pl.pallas_call(kernel, name='residual', out_shape=jax.ShapeDtypeStruct((R...  106 us

profile of v4, /device:TPU:1, one launch (start us, length us, event | category | flops | bytes accessed | tf_op | source)
XLA Modules:
  0.0 108.2 jit_solution(6248954191045566480)
XLA Ops:
  0.0 106.3 %residual.1 = bf16[768,384]{1,0:T(8,128)(2,1)} custom-call(bf16[768,384]{1,0:T(8,128)(2,1)} %bitcast.5, bf16[192,384]{1,0:T(8,128)(2,1)} %fock_ref.1, bf16[768,384]{1,0:T(8,128)(2,1)} %bitcast.6, s32[4,2,4]{2,1,0:T(2,128)} %mask_ref.1, bf16[768,384]{1,0:T(8,128)(2,1)} %bitcast.7), custom_call_target="tpu_custom_call" | custom-call | tf_op jit(solution)/shard_map/residual/pallas_call | solution.py:347
  106.3 1.9 %copy.7 = bf16[4,192,384]{2,1,0:T(8,128)(2,1)} copy(bf16[4,192,384]{2,1,0:T(8,128)(2,1)} %bitcast.4) | data formatting | bytes 1179648
